TPU v7x, 512 devices: a whole 4x4x16 slice. The times are simulated.
512 devices in a mesh: blk: 256 (over z, x, y_hi, core), head: 2 (over y_lo).
Axes of the slice: x: 4, y: 4 (y_hi: 2, y_lo: 2; y = y_hi * 2 + y_lo), z: 16, core: 2. Of those that a mesh axis runs over, the one named last changes fastest.
Arguments:
- ref_a: bfloat16 [32768, 1024], P('blk', 'head'), may hold values from -8 to 8
- val_a: bfloat16 [32768, 1024], P('blk', 'head'), may hold values from -6 to 6
- ref_b: bfloat16 [32768, 1024], P('blk', 'head'), may hold values from -8 to 8
- val_b: bfloat16 [32768, 1024], P('blk', 'head'), may hold values from -6 to 6
- w_out_a: bfloat16 [1024, 1024], P('head'), may hold values from -0.1875 to 0.1875
- w_out_b: bfloat16 [1024, 1024], P('head'), may hold values from -0.1875 to 0.1875
Outputs:
- out_a: bfloat16 [32768, 1024], P(('blk', 'head'))
- out_b: bfloat16 [32768, 1024], P(('blk', 'head'))
All inputs are finite; a program needn't handle non-finite values.
Results may differ from a plain program's by a relative error of at most 0.0055.
Values may be sent and summed in bfloat16 or wider, within the bound.
A program may use at most 64 MiB of HBM per device.

v0:
```python
import functools
import math

import jax
import jax.numpy as jnp
from jax import lax
from jax.experimental import pallas as pl
from jax.experimental.pallas import tpu as pltpu
from jax.sharding import PartitionSpec as P


ROWS = 128
HALF = 64
PAIR = 128
WIDTH = 1024
CHUNKS = 2
PIECE = WIDTH // CHUNKS
SCORE = 0.125 * math.log2(math.e)
BF16 = jnp.bfloat16
F32 = jnp.float32


def split_heads(query):
    lane = lax.broadcasted_iota(jnp.int32, (ROWS, PAIR), 1)
    query = query.astype(F32)
    zero = jnp.zeros_like(query)
    return jnp.concatenate(
        [jnp.where(lane < HALF, query, zero), jnp.where(lane < HALF, zero, query)], axis=0
    ).astype(BF16)


def pair_part(both, key, value):
    scores = lax.dot_general(key, both, (((1,), (1,)), ((), ())), preferred_element_type=F32)
    top = jnp.max(scores, axis=0, keepdims=True)
    expo = jnp.exp2((scores - top) * SCORE)
    accum = jnp.dot(value, expo.astype(BF16), preferred_element_type=F32)
    return top, jnp.sum(expo, axis=0, keepdims=True), accum[:HALF, :ROWS], accum[HALF:, ROWS:]


def merge_parts(parts):
    top = functools.reduce(jnp.maximum, [part[0] for part in parts])
    scales = [jnp.exp2((part[0] - top) * SCORE) for part in parts]
    return (
        top,
        sum(scale * part[1] for scale, part in zip(scales, parts)),
        sum(scale[:, :ROWS] * part[2] for scale, part in zip(scales, parts)),
        sum(scale[:, ROWS:] * part[3] for scale, part in zip(scales, parts)),
    )


def finish(part):
    _, total, first, second = part
    result = jnp.concatenate([first / total[:, :ROWS], second / total[:, ROWS:]], axis=0)
    return result.T.astype(BF16)


def kernel(
    count,
    ref_a,
    val_a,
    ref_b,
    val_b,
    w_a,
    w_b,
    out,
    staged,
    held,
    turned,
    weights,
    stats,
    sums,
    attn,
    gathered,
    outgoing,
    incoming,
    own,
    here_sem,
    near_sem,
    weight_sem,
    stage_sem,
    share_send,
    share_recv,
    band_send,
    band_recv,
    attn_send,
    attn_recv,
    part_send,
    part_recv,
):
    blk, head = lax.axis_index("blk"), lax.axis_index("head")
    place = lax.rem(blk, 4)
    base = blk - place
    other = 1 - head
    following = lax.rem(blk + 4, count)
    previous = lax.rem(blk + count - 4, count)
    swapped = lax.rem(place, 2) * 2 + place // 2

    herald = (place == 1) & (head == 1)
    barrier = pltpu.get_barrier_semaphore()
    for p in (0, 2, 3):
        pl.semaphore_signal(barrier, inc=1, device_id={"blk": base + p, "head": other})

    @pl.when(head == 1)
    def _():
        pl.semaphore_signal(barrier, inc=1, device_id={"blk": base + 1, "head": other})

    loads = [
        pltpu.make_async_copy(w, weights.at[side], weight_sem.at[side])
        for side, w in enumerate((w_a, w_b))
    ]
    for side, pair in enumerate(((ref_a, val_a), (ref_b, val_b))):
        for p in range(4):
            for t in range(2):
                pltpu.make_async_copy(
                    pair[t].at[:, pl.ds(p * PAIR, PAIR)], staged.at[side, p, t], stage_sem.at[side]
                ).start()
    for load in loads:
        load.start()

    @pl.when(jnp.logical_not(herald))
    def _():
        pl.semaphore_wait(barrier, 4)

    @pl.when(head == 0)
    def _():
        pl.semaphore_signal(here_sem, inc=1, device_id={"blk": base + 1, "head": other})

    @pl.when(herald)
    def _():
        pl.semaphore_wait(here_sem, 4)
        for near in (previous, following):
            pl.semaphore_signal(barrier, inc=1, device_id={"blk": near})


    def landed(ref, sem):
        pltpu.make_async_remote_copy(
            src_ref=ref, dst_ref=ref, send_sem=sem, recv_sem=sem, device_id={"head": other}
        ).wait_recv()

    def left(ref, sem):
        pltpu.make_async_remote_copy(
            src_ref=ref, dst_ref=ref, send_sem=sem, recv_sem=sem, device_id={"head": other}
        ).wait_send()

    def share(side, p):
        return pltpu.make_async_remote_copy(
            src_ref=staged.at[side, p],
            dst_ref=held.at[side, place + 1 + side],
            send_sem=share_send.at[side],
            recv_sem=share_recv.at[side, place],
            device_id={"blk": base + p, "head": other},
        )

    pltpu.make_async_copy(staged.at[1], staged.at[1], stage_sem.at[1]).wait()
    for p in range(4):
        share(1, p).start()
    pltpu.make_async_copy(staged.at[0], staged.at[0], stage_sem.at[0]).wait()

    @pl.when(jnp.logical_not(herald))
    def _():
        left(staged.at[1], share_send.at[1])

    for p in range(4):
        share(0, p).start()

    @pl.when(herald)
    def _():
        pl.semaphore_wait(barrier, 2)
        for p in range(4):
            pl.semaphore_signal(near_sem, inc=1, device_id={"blk": base + p, "head": other})
        for p in (0, 2, 3):
            pl.semaphore_signal(near_sem, inc=1, device_id={"blk": base + p})

    def wait_share(side, blocks):
        for block in blocks:
            landed(held.at[side, block + 1 + side], share_recv.at[side, block])

    bands = ((1, 4, 0, 2, True), (1, 2, 6, 1, False), (0, 4, 0, 1, True), (0, 1, 5, 2, False))

    def band(index):
        side, first, target, blocks, forward = bands[index]
        return pltpu.make_async_remote_copy(
            src_ref=held.at[side, pl.ds(first, blocks)],
            dst_ref=held.at[side, pl.ds(target, blocks)],
            send_sem=band_send,
            recv_sem=band_recv.at[index],
            device_id={"blk": following if forward else previous},
        )

    def turn(side, first, blocks):
        for position in range(first, first + blocks):
            turned[side, position] = held[side, position, 1].T

    def attn_copies(side, n):
        if n in (0, 3):
            pieces = ((n, pl.ds(0, ROWS)),)
        else:
            pieces = (
                (n, pl.ds(pl.multiple_of(other * HALF, HALF), HALF)),
                (3 - n, pl.ds(pl.multiple_of(head * HALF, HALF), HALF)),
            )
        return [
            pltpu.make_async_remote_copy(
                src_ref=attn.at[side, n, rows],
                dst_ref=gathered.at[side, place, rows],
                send_sem=attn_send.at[side],
                recv_sem=attn_recv.at[side],
                device_id={"blk": base + target, "head": other},
            )
            for target, rows in pieces
        ]

    def pairs(side, n, positions):
        both = split_heads(held[side, n + 1 + side, 0])
        return [
            pair_part(both, held[1 - side, position, 0], turned[1 - side, position])
            for position in positions
        ]

    def ready(side, n, part):
        attn[side, n] = finish(part)

    def begin(side, n, positions):
        part = merge_parts(pairs(side, n, positions))
        if len(positions) == 4:
            ready(side, n, part)
        else:
            stats[side, n, 0:1], stats[side, n, 1:2] = part[0], part[1]
            sums[side, n, :HALF], sums[side, n, HALF:] = part[2], part[3]

    def complete(side, n, positions):
        state = (
            stats[side, n, 0:1],
            stats[side, n, 1:2],
            sums[side, n, :HALF],
            sums[side, n, HALF:],
        )
        ready(side, n, merge_parts([state] + pairs(side, n, positions)))

    def give(*tasks):
        for side, n in tasks:
            for copy in attn_copies(side, n):
                copy.start()

    def pass_on(index):
        side, first, _, blocks, _ = bands[index]
        wait_share(side, range(first - 1 - side, first - 1 - side + blocks))
        band(index).start()

    @pl.when(jnp.logical_not(herald))
    def _():
        pl.semaphore_wait(near_sem, 1)

    pass_on(0)
    pass_on(1)
    wait_share(1, (1,))
    turn(1, 2, 4)
    pass_on(2)
    pass_on(3)
    wait_share(0, (2,))
    begin(0, 2, (2, 3, 4, 5))
    give((0, 2),)
    begin(0, 3, (3, 4, 5))
    begin(0, 1, (2, 3, 4))
    begin(0, 0, (2, 3))
    turn(0, 1, 4)
    begin(1, 1, (1, 2, 3, 4))
    give((1, 1),)
    begin(1, 2, (2, 3, 4))
    begin(1, 3, (3, 4))
    begin(1, 0, (1, 2, 3))
    band(1).wait_recv()
    turn(1, 6, 1)
    complete(0, 3, (6,))
    give((0, 3),)
    band(0).wait_recv()
    turn(1, 0, 2)
    complete(0, 1, (1,))
    complete(0, 0, (0, 1))
    give((0, 1), (0, 0))
    band(3).wait_recv()
    turn(0, 5, 2)
    complete(1, 2, (5,))
    complete(1, 3, (5, 6))
    give((1, 2), (1, 3))
    band(2).wait_recv()
    turn(0, 0, 1)
    complete(1, 0, (0,))
    give((1, 0),)

    mine = pl.ds(pl.multiple_of(head * HALF, HALF), HALF)
    theirs = pl.ds(pl.multiple_of(other * HALF, HALF), HALF)

    def part(side, chunk):
        return pltpu.make_async_remote_copy(
            src_ref=outgoing.at[side, chunk],
            dst_ref=incoming.at[side, chunk],
            send_sem=part_send.at[side],
            recv_sem=part_recv.at[side, chunk],
            device_id={"blk": base + swapped, "head": other},
        )

    for side in range(2):
        loads[side].wait()
        landed(gathered.at[side], attn_recv.at[side])
        rows = jnp.concatenate(
            [
                jnp.concatenate([gathered[side, p, half] for p in range(4)], axis=1)
                for half in (mine, theirs)
            ],
            axis=0,
        )
        for chunk in range(CHUNKS):
            product = jnp.dot(
                rows,
                weights[side, :, chunk * PIECE : (chunk + 1) * PIECE],
                preferred_element_type=F32,
            )
            outgoing[side, chunk] = product[HALF:].astype(BF16)
            part(side, chunk).start()
            own[side, chunk] = product[:HALF]

    @pl.when(herald)
    def _():
        left(staged.at[1], share_send.at[1])

    left(staged.at[0], share_send.at[0])
    left(held.at[0, pl.ds(0, 6)], band_send)
    for side in range(2):
        left(attn.at[side], attn_send.at[side])
        left(outgoing.at[side], part_send.at[side])

    for side in range(2):
        for chunk in range(CHUNKS):
            part(side, chunk).wait_recv()
            out[side, :, chunk * PIECE : (chunk + 1) * PIECE] = (
                own[side, chunk] + incoming[side, chunk].astype(F32)
            ).astype(BF16)


def solution(mesh):
    count = mesh.shape["blk"]

    def shards(ref_a, val_a, ref_b, val_b, w_out_a, w_out_b):
        hbm = pl.BlockSpec(memory_space=pltpu.HBM)
        vmem = pl.BlockSpec(memory_space=pltpu.VMEM)
        out = pltpu.VMEM((2, HALF, WIDTH), BF16)
        results = pl.pallas_call(
            functools.partial(kernel, count),
            out_shape=out,
            in_specs=[hbm] * 6,
            out_specs=vmem,
            scratch_shapes=[
                pltpu.VMEM((2, 4, 2, ROWS, PAIR), BF16),
                pltpu.VMEM((2, 7, 2, ROWS, PAIR), BF16),
                pltpu.VMEM((2, 7, PAIR, ROWS), BF16),
                pltpu.VMEM((2, WIDTH // 2, WIDTH), BF16),
                pltpu.VMEM((2, 4, 8, 2 * ROWS), F32),
                pltpu.VMEM((2, 4, PAIR, ROWS), F32),
                pltpu.VMEM((2, 4, ROWS, PAIR), BF16),
                pltpu.VMEM((2, 4, ROWS, PAIR), BF16),
                pltpu.VMEM((2, CHUNKS, HALF, PIECE), BF16),
                pltpu.VMEM((2, CHUNKS, HALF, PIECE), BF16),
                pltpu.VMEM((2, CHUNKS, HALF, PIECE), F32),
                pltpu.SemaphoreType.REGULAR,
                pltpu.SemaphoreType.REGULAR,
                pltpu.SemaphoreType.DMA((2,)),
                pltpu.SemaphoreType.DMA((2,)),
                pltpu.SemaphoreType.DMA((2,)),
                pltpu.SemaphoreType.DMA((2, 4)),
                pltpu.SemaphoreType.DMA,
                pltpu.SemaphoreType.DMA((4,)),
                pltpu.SemaphoreType.DMA((2,)),
                pltpu.SemaphoreType.DMA((2,)),
                pltpu.SemaphoreType.DMA((2,)),
                pltpu.SemaphoreType.DMA((2, CHUNKS)),
            ],
            compiler_params=pltpu.CompilerParams(
                collective_id=0, has_side_effects=True, vmem_limit_bytes=32 * 1024 * 1024
            ),
        )(
            *(
                pltpu.with_memory_space_constraint(array, pltpu.HBM)
                for array in (ref_a, val_a, ref_b, val_b, w_out_a, w_out_b)
            )
        )
        return results[0], results[1]

    return jax.shard_map(
        shards,
        mesh=mesh,
        in_specs=(
            P("blk", "head"),
            P("blk", "head"),
            P("blk", "head"),
            P("blk", "head"),
            P("head", None),
            P("head", None),
        ),
        out_specs=(P(("blk", "head"), None), P(("blk", "head"), None)),
        check_vma=False,
    )
```

profile of v0, /device:TPU:1, one launch (start us, length us, event | category | flops | bytes accessed | tf_op | source)
XLA Modules:
  0.0 36.3 jit_solution(15695920367704853903)
XLA Ops:
  0.6 34.9 %shard_map.77 = bf16[2,64,1024]{2,1,0:T(8,128)(2,1)S(1)} custom-call(bf16[128,512]{1,0:T(8,128)(2,1)} %ref_a.1, bf16[128,512]{1,0:T(8,128)(2,1)} %val_a.1, bf16[128,512]{1,0:T(8,128)(2,1)} %ref_b.1, bf16[128,512]{1,0:T(8,128)(2,1)} %val_b.1, bf16[512,1024]{1,0:T(8,128)(2,1)} %w_a.1, bf16[512,1024]{1,0:T(8,128)(2,1)} %w_b.1), custom_call_target="tpu_custom_call" | custom-call | tf_op jit(solution)/shard_map/pallas_call | solution.py:348
  35.6 0.7 %slice_bitcast_fusion = (bf16[64,1024]{1,0:T(8,128)(2,1)}, bf16[64,1024]{1,0:T(8,128)(2,1)}) fusion(bf16[2,64,1024]{2,1,0:T(8,128)(2,1)S(1)} %shard_map.77), kind=kLoop, calls=%fused_computation | loop fusion | bytes 524288 | tf_op jit(solution)/shard_map/squeeze | solution.py:387
where the time goes:
time: 36.4 us; the launch traced here: 36.3 us
  Pallas kernels  34.9 us (96%)
  local copies, waits for them, and re-layouts  0.72 us (2%)
  between operations  0.64 us (2%)
    pallas_call x1, Pallas kernels, shards(): pl.pallas_call(functools.partial(kernel, count), out_shape=out, in_specs=...  34.9 us

commit v1 on v0

--- a/solution.py
+++ b/solution.py
@@ -108,11 +108,11 @@
         pltpu.make_async_copy(w, weights.at[side], weight_sem.at[side])
         for side, w in enumerate((w_a, w_b))
     ]
-    for side, pair in enumerate(((ref_a, val_a), (ref_b, val_b))):
-        for p in range(4):
-            for t in range(2):
+    for side, pair in ((1, (ref_b, val_b)), (0, (ref_a, val_a))):
+        for t in range(2):
+            for p in range(4):
                 pltpu.make_async_copy(
-                    pair[t].at[:, pl.ds(p * PAIR, PAIR)], staged.at[side, p, t], stage_sem.at[side]
+                    pair[t].at[:, pl.ds(p * PAIR, PAIR)], staged.at[side, t, p], stage_sem.at[side, t]
                 ).start()
     for load in loads:
         load.start()
@@ -142,26 +142,29 @@
             src_ref=ref, dst_ref=ref, send_sem=sem, recv_sem=sem, device_id={"head": other}
         ).wait_send()
 
-    def share(side, p):
+    def share(side, t, p):
         return pltpu.make_async_remote_copy(
-            src_ref=staged.at[side, p],
-            dst_ref=held.at[side, place + 1 + side],
-            send_sem=share_send.at[side],
-            recv_sem=share_recv.at[side, place],
+            src_ref=staged.at[side, t, p],
+            dst_ref=held.at[side, t, place + 1 + side],
+            send_sem=share_send.at[side, t],
+            recv_sem=share_recv.at[side, t, place],
             device_id={"blk": base + p, "head": other},
         )
 
-    pltpu.make_async_copy(staged.at[1], staged.at[1], stage_sem.at[1]).wait()
-    for p in range(4):
-        share(1, p).start()
-    pltpu.make_async_copy(staged.at[0], staged.at[0], stage_sem.at[0]).wait()
-
-    @pl.when(jnp.logical_not(herald))
-    def _():
-        left(staged.at[1], share_send.at[1])
-
-    for p in range(4):
-        share(0, p).start()
+    def shares(side, t):
+        pltpu.make_async_copy(staged.at[side, t], staged.at[side, t], stage_sem.at[side, t]).wait()
+        for p in range(4):
+            share(side, t, p).start()
+
+    shares(1, 0)
+    shares(1, 1)
+    for t in range(2):
+
+        @pl.when(jnp.logical_not(herald))
+        def _():
+            left(staged.at[1, t], share_send.at[1, t])
+
+        shares(0, t)
 
     @pl.when(herald)
     def _():
@@ -171,25 +174,35 @@
         for p in (0, 2, 3):
             pl.semaphore_signal(near_sem, inc=1, device_id={"blk": base + p})
 
-    def wait_share(side, blocks):
+    def wait_share(side, t, blocks):
         for block in blocks:
-            landed(held.at[side, block + 1 + side], share_recv.at[side, block])
+            landed(held.at[side, t, block + 1 + side], share_recv.at[side, t, block])
 
     bands = ((1, 4, 0, 2, True), (1, 2, 6, 1, False), (0, 4, 0, 1, True), (0, 1, 5, 2, False))
 
-    def band(index):
+    def band(index, t):
         side, first, target, blocks, forward = bands[index]
         return pltpu.make_async_remote_copy(
-            src_ref=held.at[side, pl.ds(first, blocks)],
-            dst_ref=held.at[side, pl.ds(target, blocks)],
-            send_sem=band_send,
-            recv_sem=band_recv.at[index],
+            src_ref=held.at[side, t, pl.ds(first, blocks)],
+            dst_ref=held.at[side, t, pl.ds(target, blocks)],
+            send_sem=band_send.at[t],
+            recv_sem=band_recv.at[index, t],
             device_id={"blk": following if forward else previous},
         )
 
     def turn(side, first, blocks):
         for position in range(first, first + blocks):
-            turned[side, position] = held[side, position, 1].T
+            turned[side, position] = held[side, 1, position].T
+
+    def pass_on(t, *indices):
+        for index in indices:
+            side, first, _, blocks, _ = bands[index]
+            wait_share(side, t, range(first - 1 - side, first - 1 - side + blocks))
+            band(index, t).start()
+
+    def wait_band(index):
+        for t in range(2):
+            band(index, t).wait_recv()
 
     def attn_copies(side, n):
         if n in (0, 3):
@@ -211,9 +224,9 @@
         ]
 
     def pairs(side, n, positions):
-        both = split_heads(held[side, n + 1 + side, 0])
+        both = split_heads(held[side, 0, n + 1 + side])
         return [
-            pair_part(both, held[1 - side, position, 0], turned[1 - side, position])
+            pair_part(both, held[1 - side, 0, position], turned[1 - side, position])
             for position in positions
         ]
 
@@ -242,22 +255,19 @@
             for copy in attn_copies(side, n):
                 copy.start()
 
-    def pass_on(index):
-        side, first, _, blocks, _ = bands[index]
-        wait_share(side, range(first - 1 - side, first - 1 - side + blocks))
-        band(index).start()
-
     @pl.when(jnp.logical_not(herald))
     def _():
         pl.semaphore_wait(near_sem, 1)
 
-    pass_on(0)
-    pass_on(1)
-    wait_share(1, (1,))
+    pass_on(0, 0, 1)
+    pass_on(1, 0, 1)
+    for t in range(2):
+        wait_share(1, t, (1,))
     turn(1, 2, 4)
-    pass_on(2)
-    pass_on(3)
-    wait_share(0, (2,))
+    pass_on(0, 2, 3)
+    pass_on(1, 2, 3)
+    for t in range(2):
+        wait_share(0, t, (2,))
     begin(0, 2, (2, 3, 4, 5))
     give((0, 2),)
     begin(0, 3, (3, 4, 5))
@@ -269,21 +279,21 @@
     begin(1, 2, (2, 3, 4))
     begin(1, 3, (3, 4))
     begin(1, 0, (1, 2, 3))
-    band(1).wait_recv()
+    wait_band(1)
     turn(1, 6, 1)
     complete(0, 3, (6,))
     give((0, 3),)
-    band(0).wait_recv()
+    wait_band(0)
     turn(1, 0, 2)
     complete(0, 1, (1,))
     complete(0, 0, (0, 1))
     give((0, 1), (0, 0))
-    band(3).wait_recv()
+    wait_band(3)
     turn(0, 5, 2)
     complete(1, 2, (5,))
     complete(1, 3, (5, 6))
     give((1, 2), (1, 3))
-    band(2).wait_recv()
+    wait_band(2)
     turn(0, 0, 1)
     complete(1, 0, (0,))
     give((1, 0),)
@@ -322,10 +332,12 @@
 
     @pl.when(herald)
     def _():
-        left(staged.at[1], share_send.at[1])
-
-    left(staged.at[0], share_send.at[0])
-    left(held.at[0, pl.ds(0, 6)], band_send)
+        for t in range(2):
+            left(staged.at[1, t], share_send.at[1, t])
+
+    for t in range(2):
+        left(staged.at[0, t], share_send.at[0, t])
+        left(held.at[0, 0, pl.ds(0, 6)], band_send.at[t])
     for side in range(2):
         left(attn.at[side], attn_send.at[side])
         left(outgoing.at[side], part_send.at[side])
@@ -351,8 +363,8 @@
             in_specs=[hbm] * 6,
             out_specs=vmem,
             scratch_shapes=[
-                pltpu.VMEM((2, 4, 2, ROWS, PAIR), BF16),
-                pltpu.VMEM((2, 7, 2, ROWS, PAIR), BF16),
+                pltpu.VMEM((2, 2, 4, ROWS, PAIR), BF16),
+                pltpu.VMEM((2, 2, 7, ROWS, PAIR), BF16),
                 pltpu.VMEM((2, 7, PAIR, ROWS), BF16),
                 pltpu.VMEM((2, WIDTH // 2, WIDTH), BF16),
                 pltpu.VMEM((2, 4, 8, 2 * ROWS), F32),
@@ -365,11 +377,11 @@
                 pltpu.SemaphoreType.REGULAR,
                 pltpu.SemaphoreType.REGULAR,
                 pltpu.SemaphoreType.DMA((2,)),
+                pltpu.SemaphoreType.DMA((2, 2)),
+                pltpu.SemaphoreType.DMA((2, 2)),
+                pltpu.SemaphoreType.DMA((2, 2, 4)),
                 pltpu.SemaphoreType.DMA((2,)),
-                pltpu.SemaphoreType.DMA((2,)),
-                pltpu.SemaphoreType.DMA((2, 4)),
-                pltpu.SemaphoreType.DMA,
-                pltpu.SemaphoreType.DMA((4,)),
+                pltpu.SemaphoreType.DMA((4, 2)),
                 pltpu.SemaphoreType.DMA((2,)),
                 pltpu.SemaphoreType.DMA((2,)),
                 pltpu.SemaphoreType.DMA((2,)),

time: 36.4 us -> 36.1 us (level)
    pallas_call x1, Pallas kernels: 34.9 us -> 34.6 us  [shards(): pl.pallas_call(functools.partial(kernel, count), out_shape=out, in_specs=...]
where the time goes in v1:
time: 36.1 us; the launch traced here: 35.9 us
  Pallas kernels  34.6 us (96%)
  local copies, waits for them, and re-layouts  0.72 us (2%)
  between operations  0.64 us (2%)
    pallas_call x1, Pallas kernels, shards(): pl.pallas_call(functools.partial(kernel, count), out_shape=out, in_specs=...  34.6 us

profile of v1, /device:TPU:1, one launch (start us, length us, event | category | flops | bytes accessed | tf_op | source)
XLA Modules:
  0.0 35.9 jit_solution(2884633969939167957)
XLA Ops:
  0.6 34.6 %shard_map.77 = bf16[2,64,1024]{2,1,0:T(8,128)(2,1)S(1)} custom-call(bf16[128,512]{1,0:T(8,128)(2,1)} %ref_a.1, bf16[128,512]{1,0:T(8,128)(2,1)} %val_a.1, bf16[128,512]{1,0:T(8,128)(2,1)} %ref_b.1, bf16[128,512]{1,0:T(8,128)(2,1)} %val_b.1, bf16[512,1024]{1,0:T(8,128)(2,1)} %w_a.1, bf16[512,1024]{1,0:T(8,128)(2,1)} %w_b.1), custom_call_target="tpu_custom_call" | custom-call | tf_op jit(solution)/shard_map/pallas_call | solution.py:360
  35.2 0.7 %slice_bitcast_fusion = (bf16[64,1024]{1,0:T(8,128)(2,1)}, bf16[64,1024]{1,0:T(8,128)(2,1)}) fusion(bf16[2,64,1024]{2,1,0:T(8,128)(2,1)S(1)} %shard_map.77), kind=kLoop, calls=%fused_computation | loop fusion | bytes 524288 | tf_op jit(solution)/shard_map/squeeze | solution.py:399

commit v2 on v1

--- a/solution.py
+++ b/solution.py
@@ -108,12 +108,11 @@
         pltpu.make_async_copy(w, weights.at[side], weight_sem.at[side])
         for side, w in enumerate((w_a, w_b))
     ]
-    for side, pair in ((1, (ref_b, val_b)), (0, (ref_a, val_a))):
-        for t in range(2):
-            for p in range(4):
-                pltpu.make_async_copy(
-                    pair[t].at[:, pl.ds(p * PAIR, PAIR)], staged.at[side, t, p], stage_sem.at[side, t]
-                ).start()
+    for t, source in enumerate((ref_a, val_a)):
+        for p in range(4):
+            pltpu.make_async_copy(
+                source.at[:, pl.ds(p * PAIR, PAIR)], staged.at[t, p], stage_sem.at[t]
+            ).start()
     for load in loads:
         load.start()
 
@@ -144,7 +143,7 @@
 
     def share(side, t, p):
         return pltpu.make_async_remote_copy(
-            src_ref=staged.at[side, t, p],
+            src_ref=(ref_b, val_b)[t].at[:, pl.ds(p * PAIR, PAIR)] if side else staged.at[t, p],
             dst_ref=held.at[side, t, place + 1 + side],
             send_sem=share_send.at[side, t],
             recv_sem=share_recv.at[side, t, place],
@@ -152,7 +151,6 @@
         )
 
     def shares(side, t):
-        pltpu.make_async_copy(staged.at[side, t], staged.at[side, t], stage_sem.at[side, t]).wait()
         for p in range(4):
             share(side, t, p).start()
 
@@ -162,8 +160,9 @@
 
         @pl.when(jnp.logical_not(herald))
         def _():
-            left(staged.at[1, t], share_send.at[1, t])
-
+            left(staged.at[t], share_send.at[1, t])
+
+        pltpu.make_async_copy(staged.at[t], staged.at[t], stage_sem.at[t]).wait()
         shares(0, t)
 
     @pl.when(herald)
@@ -333,10 +332,10 @@
     @pl.when(herald)
     def _():
         for t in range(2):
-            left(staged.at[1, t], share_send.at[1, t])
+            left(staged.at[t], share_send.at[1, t])
 
     for t in range(2):
-        left(staged.at[0, t], share_send.at[0, t])
+        left(staged.at[t], share_send.at[0, t])
         left(held.at[0, 0, pl.ds(0, 6)], band_send.at[t])
     for side in range(2):
         left(attn.at[side], attn_send.at[side])
@@ -363,7 +362,7 @@
             in_specs=[hbm] * 6,
             out_specs=vmem,
             scratch_shapes=[
-                pltpu.VMEM((2, 2, 4, ROWS, PAIR), BF16),
+                pltpu.VMEM((2, 4, ROWS, PAIR), BF16),
                 pltpu.VMEM((2, 2, 7, ROWS, PAIR), BF16),
                 pltpu.VMEM((2, 7, PAIR, ROWS), BF16),
                 pltpu.VMEM((2, WIDTH // 2, WIDTH), BF16),
@@ -377,7 +376,7 @@
                 pltpu.SemaphoreType.REGULAR,
                 pltpu.SemaphoreType.REGULAR,
                 pltpu.SemaphoreType.DMA((2,)),
-                pltpu.SemaphoreType.DMA((2, 2)),
+                pltpu.SemaphoreType.DMA((2,)),
                 pltpu.SemaphoreType.DMA((2, 2)),
                 pltpu.SemaphoreType.DMA((2, 2, 4)),
                 pltpu.SemaphoreType.DMA((2,)),

time: 36.1 us -> 36.3 us (level)
  no operation moved by 1% of the time
where the time goes in v2:
time: 36.3 us; the launch traced here: 36.2 us
  Pallas kernels  34.9 us (96%)
  local copies, waits for them, and re-layouts  0.72 us (2%)
  between operations  0.64 us (2%)
    pallas_call x1, Pallas kernels, shards(): pl.pallas_call(functools.partial(kernel, count), out_shape=out, in_specs=...  34.9 us

profile of v2, /device:TPU:1, one launch (start us, length us, event | category | flops | bytes accessed | tf_op | source)
XLA Modules:
  0.0 36.2 jit_solution(5755979352254883994)
XLA Ops:
  0.6 34.9 %shard_map.77 = bf16[2,64,1024]{2,1,0:T(8,128)(2,1)S(1)} custom-call(bf16[128,512]{1,0:T(8,128)(2,1)} %ref_a.1, bf16[128,512]{1,0:T(8,128)(2,1)} %val_a.1, bf16[128,512]{1,0:T(8,128)(2,1)} %ref_b.1, bf16[128,512]{1,0:T(8,128)(2,1)} %val_b.1, bf16[512,1024]{1,0:T(8,128)(2,1)} %w_a.1, bf16[512,1024]{1,0:T(8,128)(2,1)} %w_b.1), custom_call_target="tpu_custom_call" | custom-call | tf_op jit(solution)/shard_map/pallas_call | solution.py:359
  35.5 0.7 %slice_bitcast_fusion = (bf16[64,1024]{1,0:T(8,128)(2,1)}, bf16[64,1024]{1,0:T(8,128)(2,1)}) fusion(bf16[2,64,1024]{2,1,0:T(8,128)(2,1)S(1)} %shard_map.77), kind=kLoop, calls=%fused_computation | loop fusion | bytes 524288 | tf_op jit(solution)/shard_map/squeeze | solution.py:398

commit v3 on v1

--- a/solution.py
+++ b/solution.py
@@ -11,6 +11,7 @@
 
 ROWS = 128
 HALF = 64
+QUARTER = 32
 PAIR = 128
 WIDTH = 1024
 CHUNKS = 2
@@ -93,7 +94,6 @@
     other = 1 - head
     following = lax.rem(blk + 4, count)
     previous = lax.rem(blk + count - 4, count)
-    swapped = lax.rem(place, 2) * 2 + place // 2
 
     herald = (place == 1) & (head == 1)
     barrier = pltpu.get_barrier_semaphore()
@@ -205,22 +205,20 @@
             band(index, t).wait_recv()
 
     def attn_copies(side, n):
-        if n in (0, 3):
-            pieces = ((n, pl.ds(0, ROWS)),)
-        else:
-            pieces = (
-                (n, pl.ds(pl.multiple_of(other * HALF, HALF), HALF)),
-                (3 - n, pl.ds(pl.multiple_of(head * HALF, HALF), HALF)),
-            )
+        start, last = divmod(n, 2)
+        pieces = [(n, other * HALF, 0, HALF)] + [
+            (2 * part + last, head * HALF + part * QUARTER, HALF + start * QUARTER, QUARTER)
+            for part in range(2)
+        ]
         return [
             pltpu.make_async_remote_copy(
-                src_ref=attn.at[side, n, rows],
-                dst_ref=gathered.at[side, place, rows],
+                src_ref=attn.at[side, n, pl.ds(pl.multiple_of(first, QUARTER), rows)],
+                dst_ref=gathered.at[side, place, pl.ds(target, rows)],
                 send_sem=attn_send.at[side],
                 recv_sem=attn_recv.at[side],
-                device_id={"blk": base + target, "head": other},
+                device_id={"blk": base + owner, "head": other},
             )
-            for target, rows in pieces
+            for owner, first, target, rows in pieces
         ]
 
     def pairs(side, n, positions):
@@ -298,28 +296,23 @@
     complete(1, 0, (0,))
     give((1, 0),)
 
-    mine = pl.ds(pl.multiple_of(head * HALF, HALF), HALF)
-    theirs = pl.ds(pl.multiple_of(other * HALF, HALF), HALF)
-
-    def part(side, chunk):
+    start, last = place // 2, lax.rem(place, 2)
+
+    def part(side, chunk, piece):
         return pltpu.make_async_remote_copy(
-            src_ref=outgoing.at[side, chunk],
-            dst_ref=incoming.at[side, chunk],
+            src_ref=outgoing.at[side, chunk, pl.ds(piece * QUARTER, QUARTER)],
+            dst_ref=incoming.at[
+                side, chunk, pl.ds(pl.multiple_of(start * QUARTER, QUARTER), QUARTER)
+            ],
             send_sem=part_send.at[side],
             recv_sem=part_recv.at[side, chunk],
-            device_id={"blk": base + swapped, "head": other},
+            device_id={"blk": base + 2 * piece + last, "head": other},
         )
 
     for side in range(2):
         loads[side].wait()
         landed(gathered.at[side], attn_recv.at[side])
-        rows = jnp.concatenate(
-            [
-                jnp.concatenate([gathered[side, p, half] for p in range(4)], axis=1)
-                for half in (mine, theirs)
-            ],
-            axis=0,
-        )
+        rows = jnp.concatenate([gathered[side, p] for p in range(4)], axis=1)
         for chunk in range(CHUNKS):
             product = jnp.dot(
                 rows,
@@ -327,7 +320,8 @@
                 preferred_element_type=F32,
             )
             outgoing[side, chunk] = product[HALF:].astype(BF16)
-            part(side, chunk).start()
+            for piece in range(2):
+                part(side, chunk, piece).start()
             own[side, chunk] = product[:HALF]
 
     @pl.when(herald)
@@ -344,7 +338,7 @@
 
     for side in range(2):
         for chunk in range(CHUNKS):
-            part(side, chunk).wait_recv()
+            landed(incoming.at[side, chunk], part_recv.at[side, chunk])
             out[side, :, chunk * PIECE : (chunk + 1) * PIECE] = (
                 own[side, chunk] + incoming[side, chunk].astype(F32)
             ).astype(BF16)

time: 36.1 us -> 35.1 us (0.972)
  Pallas kernels: 34.6 us -> 33.6 us
    pallas_call x1, Pallas kernels: 34.6 us -> 33.6 us  [shards(): pl.pallas_call(functools.partial(kernel, count), out_shape=out, in_specs=...]
where the time goes in v3:
time: 35.1 us; the launch traced here: 35 us
  Pallas kernels  33.6 us (96%)
  local copies, waits for them, and re-layouts  0.72 us (2%)
  between operations  0.64 us (2%)
    pallas_call x1, Pallas kernels, shards(): pl.pallas_call(functools.partial(kernel, count), out_shape=out, in_specs=...  33.6 us
    squeeze x1, local copies, waits for them, and re-layouts, shards(): return (results[0], results[1])  0.72 us

profile of v3, /device:TPU:1, one launch (start us, length us, event | category | flops | bytes accessed | tf_op | source)
XLA Modules:
  0.0 35.0 jit_solution(1401348004131910468)
XLA Ops:
  0.6 33.6 %shard_map.77 = bf16[2,64,1024]{2,1,0:T(8,128)(2,1)S(1)} custom-call(bf16[128,512]{1,0:T(8,128)(2,1)} %ref_a.1, bf16[128,512]{1,0:T(8,128)(2,1)} %val_a.1, bf16[128,512]{1,0:T(8,128)(2,1)} %ref_b.1, bf16[128,512]{1,0:T(8,128)(2,1)} %val_b.1, bf16[512,1024]{1,0:T(8,128)(2,1)} %w_a.1, bf16[512,1024]{1,0:T(8,128)(2,1)} %w_b.1), custom_call_target="tpu_custom_call" | custom-call | tf_op jit(solution)/shard_map/pallas_call | solution.py:354
  34.2 0.7 %slice_bitcast_fusion = (bf16[64,1024]{1,0:T(8,128)(2,1)}, bf16[64,1024]{1,0:T(8,128)(2,1)}) fusion(bf16[2,64,1024]{2,1,0:T(8,128)(2,1)S(1)} %shard_map.77), kind=kLoop, calls=%fused_computation | loop fusion | bytes 524288 | tf_op jit(solution)/shard_map/squeeze | solution.py:393

commit v4 on v3

--- a/solution.py
+++ b/solution.py
@@ -277,25 +277,6 @@
     begin(1, 2, (2, 3, 4))
     begin(1, 3, (3, 4))
     begin(1, 0, (1, 2, 3))
-    wait_band(1)
-    turn(1, 6, 1)
-    complete(0, 3, (6,))
-    give((0, 3),)
-    wait_band(0)
-    turn(1, 0, 2)
-    complete(0, 1, (1,))
-    complete(0, 0, (0, 1))
-    give((0, 1), (0, 0))
-    wait_band(3)
-    turn(0, 5, 2)
-    complete(1, 2, (5,))
-    complete(1, 3, (5, 6))
-    give((1, 2), (1, 3))
-    wait_band(2)
-    turn(0, 0, 1)
-    complete(1, 0, (0,))
-    give((1, 0),)
-
     start, last = place // 2, lax.rem(place, 2)
 
     def part(side, chunk, piece):
@@ -309,7 +290,7 @@
             device_id={"blk": base + 2 * piece + last, "head": other},
         )
 
-    for side in range(2):
+    def project(side):
         loads[side].wait()
         landed(gathered.at[side], attn_recv.at[side])
         rows = jnp.concatenate([gathered[side, p] for p in range(4)], axis=1)
@@ -323,6 +304,36 @@
             for piece in range(2):
                 part(side, chunk, piece).start()
             own[side, chunk] = product[:HALF]
+
+    wait_band(1)
+    turn(1, 6, 1)
+    complete(0, 3, (6,))
+    wait_band(3)
+    turn(0, 5, 2)
+    complete(1, 2, (5,))
+    complete(1, 3, (5, 6))
+    give((0, 3), (1, 2), (1, 3))
+    wait_band(0)
+    turn(1, 1, 1)
+    complete(0, 1, (1,))
+    give((0, 1),)
+    turn(1, 0, 1)
+    complete(0, 0, (0, 1))
+    give((0, 0),)
+
+    @pl.when(last == 1)
+    def _():
+        project(1)
+
+    wait_band(2)
+    turn(0, 0, 1)
+    complete(1, 0, (0,))
+    give((1, 0),)
+    project(0)
+
+    @pl.when(last == 0)
+    def _():
+        project(1)
 
     @pl.when(herald)
     def _():

time: 35.1 us -> 33.1 us (0.943)
  Pallas kernels: 33.6 us -> 31.5 us
    pallas_call x1, Pallas kernels: 33.6 us -> 31.5 us  [shards(): pl.pallas_call(functools.partial(kernel, count), out_shape=out, in_specs=...]
where the time goes in v4:
time: 33.1 us; the launch traced here: 32.8 us
  Pallas kernels  31.5 us (95%)
  local copies, waits for them, and re-layouts  0.72 us (2%)
  between operations  0.64 us (2%)
    pallas_call x1, Pallas kernels, shards(): pl.pallas_call(functools.partial(kernel, count), out_shape=out, in_specs=...  31.5 us
    squeeze x1, local copies, waits for them, and re-layouts, shards(): return (results[0], results[1])  0.72 us

profile of v4, /device:TPU:1, one launch (start us, length us, event | category | flops | bytes accessed | tf_op | source)
XLA Modules:
  0.0 32.8 jit_solution(9462053921844332506)
XLA Ops:
  0.6 31.5 %shard_map.77 = bf16[2,64,1024]{2,1,0:T(8,128)(2,1)S(1)} custom-call(bf16[128,512]{1,0:T(8,128)(2,1)} %ref_a.1, bf16[128,512]{1,0:T(8,128)(2,1)} %val_a.1, bf16[128,512]{1,0:T(8,128)(2,1)} %ref_b.1, bf16[128,512]{1,0:T(8,128)(2,1)} %val_b.1, bf16[512,1024]{1,0:T(8,128)(2,1)} %w_a.1, bf16[512,1024]{1,0:T(8,128)(2,1)} %w_b.1), custom_call_target="tpu_custom_call" | custom-call | tf_op jit(solution)/shard_map/pallas_call | solution.py:365
  32.1 0.7 %slice_bitcast_fusion = (bf16[64,1024]{1,0:T(8,128)(2,1)}, bf16[64,1024]{1,0:T(8,128)(2,1)}) fusion(bf16[2,64,1024]{2,1,0:T(8,128)(2,1)S(1)} %shard_map.77), kind=kLoop, calls=%fused_computation | loop fusion | bytes 524288 | tf_op jit(solution)/shard_map/squeeze | solution.py:404

commit v5 on v4

--- a/solution.py
+++ b/solution.py
@@ -76,7 +76,8 @@
     incoming,
     own,
     here_sem,
-    near_sem,
+    after_sem,
+    before_sem,
     weight_sem,
     stage_sem,
     share_send,
@@ -95,14 +96,17 @@
     following = lax.rem(blk + 4, count)
     previous = lax.rem(blk + count - 4, count)
 
-    herald = (place == 1) & (head == 1)
+    fore = (place == 1) & (head == 1)
+    aft = (place == 0) & (head == 1)
+    herald = (place < 2) & (head == 1)
     barrier = pltpu.get_barrier_semaphore()
-    for p in (0, 2, 3):
+    for p in (2, 3):
         pl.semaphore_signal(barrier, inc=1, device_id={"blk": base + p, "head": other})
 
     @pl.when(head == 1)
     def _():
-        pl.semaphore_signal(barrier, inc=1, device_id={"blk": base + 1, "head": other})
+        for p in (0, 1):
+            pl.semaphore_signal(barrier, inc=1, device_id={"blk": base + p, "head": other})
 
     loads = [
         pltpu.make_async_copy(w, weights.at[side], weight_sem.at[side])
@@ -123,13 +127,20 @@
 
     @pl.when(head == 0)
     def _():
-        pl.semaphore_signal(here_sem, inc=1, device_id={"blk": base + 1, "head": other})
+        for p in (0, 1):
+            pl.semaphore_signal(here_sem, inc=1, device_id={"blk": base + p, "head": other})
 
     @pl.when(herald)
     def _():
         pl.semaphore_wait(here_sem, 4)
-        for near in (previous, following):
-            pl.semaphore_signal(barrier, inc=1, device_id={"blk": near})
+
+    @pl.when(fore)
+    def _():
+        pl.semaphore_signal(barrier, inc=1, device_id={"blk": following - 1})
+
+    @pl.when(aft)
+    def _():
+        pl.semaphore_signal(barrier, inc=1, device_id={"blk": previous + 1})
 
 
     def landed(ref, sem):
@@ -166,13 +177,20 @@
 
         shares(0, t)
 
-    @pl.when(herald)
-    def _():
-        pl.semaphore_wait(barrier, 2)
+    def tell(sem, places):
+        pl.semaphore_wait(barrier, 1)
         for p in range(4):
-            pl.semaphore_signal(near_sem, inc=1, device_id={"blk": base + p, "head": other})
-        for p in (0, 2, 3):
-            pl.semaphore_signal(near_sem, inc=1, device_id={"blk": base + p})
+            pl.semaphore_signal(sem, inc=1, device_id={"blk": base + p, "head": other})
+        for p in places:
+            pl.semaphore_signal(sem, inc=1, device_id={"blk": base + p})
+
+    @pl.when(fore)
+    def _():
+        tell(after_sem, (0, 2, 3))
+
+    @pl.when(aft)
+    def _():
+        tell(before_sem, (1, 2, 3))
 
     def wait_share(side, t, blocks):
         for block in blocks:
@@ -253,12 +271,19 @@
             for copy in attn_copies(side, n):
                 copy.start()
 
-    @pl.when(jnp.logical_not(herald))
-    def _():
-        pl.semaphore_wait(near_sem, 1)
-
-    pass_on(0, 0, 1)
-    pass_on(1, 0, 1)
+    @pl.when(jnp.logical_not(fore))
+    def _():
+        pl.semaphore_wait(after_sem, 1)
+
+    pass_on(0, 0)
+    pass_on(1, 0)
+
+    @pl.when(jnp.logical_not(aft))
+    def _():
+        pl.semaphore_wait(before_sem, 1)
+
+    pass_on(0, 1)
+    pass_on(1, 1)
     for t in range(2):
         wait_share(1, t, (1,))
     turn(1, 2, 4)
@@ -381,6 +406,7 @@
                 pltpu.VMEM((2, CHUNKS, HALF, PIECE), F32),
                 pltpu.SemaphoreType.REGULAR,
                 pltpu.SemaphoreType.REGULAR,
+                pltpu.SemaphoreType.REGULAR,
                 pltpu.SemaphoreType.DMA((2,)),
                 pltpu.SemaphoreType.DMA((2, 2)),
                 pltpu.SemaphoreType.DMA((2, 2)),

time: 33.1 us -> 33.4 us (level)
  the two profiles are of different devices: /device:TPU:1 before, /device:TPU:8 now
where the time goes in v5:
time: 33.4 us; the launch traced here: 33.2 us
  Pallas kernels  31.9 us (96%)
  local copies, waits for them, and re-layouts  0.72 us (2%)
  between operations  0.64 us (2%)
    pallas_call x1, Pallas kernels, shards(): pl.pallas_call(functools.partial(kernel, count), out_shape=out, in_specs=...  31.9 us
    squeeze x1, local copies, waits for them, and re-layouts, shards(): return (results[0], results[1])  0.72 us

profile of v5, /device:TPU:8, one launch (start us, length us, event | category | flops | bytes accessed | tf_op | source)
XLA Modules:
  0.0 33.2 jit_solution(6222603969158499508)
XLA Ops:
  0.6 31.9 %shard_map.77 = bf16[2,64,1024]{2,1,0:T(8,128)(2,1)S(1)} custom-call(bf16[128,512]{1,0:T(8,128)(2,1)} %ref_a.1, bf16[128,512]{1,0:T(8,128)(2,1)} %val_a.1, bf16[128,512]{1,0:T(8,128)(2,1)} %ref_b.1, bf16[128,512]{1,0:T(8,128)(2,1)} %val_b.1, bf16[512,1024]{1,0:T(8,128)(2,1)} %w_a.1, bf16[512,1024]{1,0:T(8,128)(2,1)} %w_b.1), custom_call_target="tpu_custom_call" | custom-call | tf_op jit(solution)/shard_map/pallas_call | solution.py:390
  32.5 0.7 %slice_bitcast_fusion = (bf16[64,1024]{1,0:T(8,128)(2,1)}, bf16[64,1024]{1,0:T(8,128)(2,1)}) fusion(bf16[2,64,1024]{2,1,0:T(8,128)(2,1)S(1)} %shard_map.77), kind=kLoop, calls=%fused_computation | loop fusion | bytes 524288 | tf_op jit(solution)/shard_map/squeeze | solution.py:430

commit v6 on v4

--- a/solution.py
+++ b/solution.py
@@ -96,6 +96,7 @@
     previous = lax.rem(blk + count - 4, count)
 
     herald = (place == 1) & (head == 1)
+    holds_back = (place == 2) & (base + 4 == count)
     barrier = pltpu.get_barrier_semaphore()
     for p in (0, 2, 3):
         pl.semaphore_signal(barrier, inc=1, device_id={"blk": base + p, "head": other})
@@ -164,7 +165,9 @@
         def _():
             left(staged.at[1, t], share_send.at[1, t])
 
-        shares(0, t)
+        @pl.when(jnp.logical_not(holds_back))
+        def _():
+            shares(0, t)
 
     @pl.when(herald)
     def _():
@@ -262,7 +265,14 @@
     for t in range(2):
         wait_share(1, t, (1,))
     turn(1, 2, 4)
-    pass_on(0, 2, 3)
+    pass_on(0, 2)
+
+    @pl.when(holds_back)
+    def _():
+        for t in range(2):
+            shares(0, t)
+
+    pass_on(0, 3)
     pass_on(1, 2, 3)
     for t in range(2):
         wait_share(0, t, (2,))
@@ -324,15 +334,16 @@
     @pl.when(last == 1)
     def _():
         project(1)
+        project(0)
 
     wait_band(2)
     turn(0, 0, 1)
     complete(1, 0, (0,))
     give((1, 0),)
-    project(0)
 
     @pl.when(last == 0)
     def _():
+        project(0)
         project(1)
 
     @pl.when(herald)

time: 33.1 us -> 36 us (1.088)
  the two profiles are of different devices: /device:TPU:1 before, /device:TPU:2 now
where the time goes in v6:
time: 36 us; the launch traced here: 35.8 us
  Pallas kernels  34.5 us (96%)
  local copies, waits for them, and re-layouts  0.72 us (2%)
  between operations  0.64 us (2%)
    pallas_call x1, Pallas kernels, shards(): pl.pallas_call(functools.partial(kernel, count), out_shape=out, in_specs=...  34.5 us

profile of v6, /device:TPU:2, one launch (start us, length us, event | category | flops | bytes accessed | tf_op | source)
XLA Modules:
  0.0 35.8 jit_solution(3188572178922827993)
XLA Ops:
  0.6 34.5 %shard_map.77 = bf16[2,64,1024]{2,1,0:T(8,128)(2,1)S(1)} custom-call(bf16[128,512]{1,0:T(8,128)(2,1)} %ref_a.1, bf16[128,512]{1,0:T(8,128)(2,1)} %val_a.1, bf16[128,512]{1,0:T(8,128)(2,1)} %ref_b.1, bf16[128,512]{1,0:T(8,128)(2,1)} %val_b.1, bf16[512,1024]{1,0:T(8,128)(2,1)} %w_a.1, bf16[512,1024]{1,0:T(8,128)(2,1)} %w_b.1), custom_call_target="tpu_custom_call" | custom-call | tf_op jit(solution)/shard_map/pallas_call | solution.py:376
  35.1 0.7 %slice_bitcast_fusion = (bf16[64,1024]{1,0:T(8,128)(2,1)}, bf16[64,1024]{1,0:T(8,128)(2,1)}) fusion(bf16[2,64,1024]{2,1,0:T(8,128)(2,1)S(1)} %shard_map.77), kind=kLoop, calls=%fused_computation | loop fusion | bytes 524288 | tf_op jit(solution)/shard_map/squeeze | solution.py:415

commit v7 on v6

--- a/solution.py
+++ b/solution.py
@@ -334,16 +334,15 @@
     @pl.when(last == 1)
     def _():
         project(1)
-        project(0)
 
     wait_band(2)
     turn(0, 0, 1)
     complete(1, 0, (0,))
     give((1, 0),)
+    project(0)
 
     @pl.when(last == 0)
     def _():
-        project(0)
         project(1)
 
     @pl.when(herald)

time: 36 us -> 33.1 us (0.919)
  the two profiles are of different devices: /device:TPU:2 before, /device:TPU:1 now
where the time goes in v7:
time: 33.1 us; the launch traced here: 32.8 us
  Pallas kernels  31.5 us (95%)
  local copies, waits for them, and re-layouts  0.72 us (2%)
  between operations  0.64 us (2%)
    pallas_call x1, Pallas kernels, shards(): pl.pallas_call(functools.partial(kernel, count), out_shape=out, in_specs=...  31.5 us
    squeeze x1, local copies, waits for them, and re-layouts, shards(): return (results[0], results[1])  0.72 us

profile of v7, /device:TPU:1, one launch (start us, length us, event | category | flops | bytes accessed | tf_op | source)
XLA Modules:
  0.0 32.8 jit_solution(15140995187577217085)
XLA Ops:
  0.6 31.5 %shard_map.77 = bf16[2,64,1024]{2,1,0:T(8,128)(2,1)S(1)} custom-call(bf16[128,512]{1,0:T(8,128)(2,1)} %ref_a.1, bf16[128,512]{1,0:T(8,128)(2,1)} %val_a.1, bf16[128,512]{1,0:T(8,128)(2,1)} %ref_b.1, bf16[128,512]{1,0:T(8,128)(2,1)} %val_b.1, bf16[512,1024]{1,0:T(8,128)(2,1)} %w_a.1, bf16[512,1024]{1,0:T(8,128)(2,1)} %w_b.1), custom_call_target="tpu_custom_call" | custom-call | tf_op jit(solution)/shard_map/pallas_call | solution.py:375
  32.1 0.7 %slice_bitcast_fusion = (bf16[64,1024]{1,0:T(8,128)(2,1)}, bf16[64,1024]{1,0:T(8,128)(2,1)}) fusion(bf16[2,64,1024]{2,1,0:T(8,128)(2,1)S(1)} %shard_map.77), kind=kLoop, calls=%fused_computation | loop fusion | bytes 524288 | tf_op jit(solution)/shard_map/squeeze | solution.py:414

commit v8 on v7

--- a/solution.py
+++ b/solution.py
@@ -14,7 +14,7 @@
 QUARTER = 32
 PAIR = 128
 WIDTH = 1024
-CHUNKS = 2
+CHUNKS = 4
 PIECE = WIDTH // CHUNKS
 SCORE = 0.125 * math.log2(math.e)
 BF16 = jnp.bfloat16

time: 33.1 us -> 33.4 us (level)
  no operation moved by 1% of the time
where the time goes in v8:
time: 33.4 us; the launch traced here: 33 us
  Pallas kernels  31.6 us (95%)
  local copies, waits for them, and re-layouts  0.72 us (2%)
  between operations  0.64 us (2%)
    pallas_call x1, Pallas kernels, shards(): pl.pallas_call(functools.partial(kernel, count), out_shape=out, in_specs=...  31.6 us
    squeeze x1, local copies, waits for them, and re-layouts, shards(): return (results[0], results[1])  0.72 us

profile of v8, /device:TPU:1, one launch (start us, length us, event | category | flops | bytes accessed | tf_op | source)
XLA Modules:
  0.0 33.0 jit_solution(9973832921666879340)
XLA Ops:
  0.6 31.6 %shard_map.77 = bf16[2,64,1024]{2,1,0:T(8,128)(2,1)S(1)} custom-call(bf16[128,512]{1,0:T(8,128)(2,1)} %ref_a.1, bf16[128,512]{1,0:T(8,128)(2,1)} %val_a.1, bf16[128,512]{1,0:T(8,128)(2,1)} %ref_b.1, bf16[128,512]{1,0:T(8,128)(2,1)} %val_b.1, bf16[512,1024]{1,0:T(8,128)(2,1)} %w_a.1, bf16[512,1024]{1,0:T(8,128)(2,1)} %w_b.1), custom_call_target="tpu_custom_call" | custom-call | tf_op jit(solution)/shard_map/pallas_call | solution.py:375
  32.2 0.7 %slice_bitcast_fusion = (bf16[64,1024]{1,0:T(8,128)(2,1)}, bf16[64,1024]{1,0:T(8,128)(2,1)}) fusion(bf16[2,64,1024]{2,1,0:T(8,128)(2,1)S(1)} %shard_map.77), kind=kLoop, calls=%fused_computation | loop fusion | bytes 524288 | tf_op jit(solution)/shard_map/squeeze | solution.py:414
